TPU v7x, 256 devices: a whole 4x4x8 slice. The times are simulated.
256 devices in a mesh: ctx: 64 (over z, x, core), head: 4 (over y).
Axes of the slice: x: 4, y: 4, z: 8, core: 2. Of those that a mesh axis runs over, the one named last changes fastest.
Arguments:
- queries: bfloat16 [12288, 16384], P('ctx', 'head'), may hold values from -16 to 16
- keys: bfloat16 [12288, 1024], P('ctx', 'head'), may hold values from -16 to 16
- values: bfloat16 [12288, 1024], P('ctx', 'head'), may hold values from -6 to 6
- doc_lengths: int32 [128], replicated, may hold values from 1 to 2880, 12288 in all
Outputs:
- attended: bfloat16 [12288, 16384], P(('ctx', 'head'))
Inputs may be any that keep to these rules, and one draw needn't show every extreme that they name: `doc_lengths`: the longest document has exactly 2880 tokens.
All inputs are finite; a program needn't handle non-finite values.
Results may differ from a plain program's by a relative error of at most 0.0029.
Values may be sent and summed in bfloat16 or wider, within the bound.
A program may use at most 64 MiB of HBM per device.

v0:
```python
import jax
import jax.numpy as jnp
from jax import lax
from jax.sharding import PartitionSpec as P

HEAD_SIZE = 128


def passed_along(value, axis, steps):
    count = lax.axis_size(axis)
    leading, last = (max(0, -steps), min(count, count - steps))
    return lax.ppermute(value, axis, [(source, source + steps) for source in range(leading, last)])


def attend_group(query_part, key_part, value_part, allowed):
    scores = jnp.einsum(
        "qhd,kd->hqk", query_part, key_part, preferred_element_type=jnp.float32
    ) * HEAD_SIZE ** (-0.5)
    scores = jnp.where(allowed[None], scores, -1e30)
    highest = jnp.max(scores, axis=-1, keepdims=True)
    probs = jnp.where(allowed[None], jnp.exp(scores - highest), 0.0)
    totals = jnp.sum(probs, axis=-1)
    rounded = probs.astype(jnp.bfloat16)
    mixed = jnp.einsum("hqk,kd->qhd", rounded, value_part, preferred_element_type=jnp.float32)
    return (mixed / jnp.transpose(totals)[:, :, None]).astype(jnp.bfloat16)


def document_ids(doc_ends, positions):
    return jnp.sum((doc_ends[None, :] <= positions[:, None]).astype(jnp.int32), axis=1)


def per_device(queries, keys, values, doc_lengths):
    tok_rows = queries.shape[0]
    width_of_keys = keys.shape[1]
    hop_count = lax.axis_size("ctx") // 4
    ctx_place = lax.axis_index("ctx")
    own_block = jnp.stack([keys, values])
    window = jnp.concatenate(
        [jnp.zeros((2, (hop_count - 1) * tok_rows, width_of_keys), own_block.dtype), own_block],
        axis=1,
    )

    def relay_step(hop_index, carry_pair):
        collected, moving = carry_pair
        moving = passed_along(moving, "ctx", 1)
        slot_start = (hop_count - 2 - hop_index) * tok_rows
        collected = lax.dynamic_update_slice_in_dim(collected, moving, slot_start, 1)
        return (collected, moving)

    window, moving = lax.fori_loop(0, hop_count - 1, relay_step, (window, own_block))
    doc_ends = jnp.cumsum(doc_lengths)
    query_pos = ctx_place * tok_rows + jnp.arange(tok_rows, dtype=jnp.int32)
    key_pos = (ctx_place - hop_count + 1) * tok_rows + jnp.arange(
        hop_count * tok_rows, dtype=jnp.int32
    )
    query_docs = document_ids(doc_ends, query_pos)
    key_docs = jnp.where(key_pos >= 0, document_ids(doc_ends, key_pos), -1)
    allowed = (key_docs[None, :] == query_docs[:, None]) & (key_pos[None, :] <= query_pos[:, None])
    groups = width_of_keys // HEAD_SIZE
    per_group = queries.shape[1] // HEAD_SIZE // groups
    heads_item = 4
    item_count = groups * per_group // heads_item
    query_items = jnp.moveaxis(queries.reshape(tok_rows, item_count, heads_item, HEAD_SIZE), 1, 0)
    key_heads = window[0].reshape(hop_count * tok_rows, groups, HEAD_SIZE)
    value_heads = window[1].reshape(hop_count * tok_rows, groups, HEAD_SIZE)

    def one_item(item_index):
        group_index = item_index // (per_group // heads_item)
        return attend_group(
            query_items[item_index], key_heads[:, group_index], value_heads[:, group_index], allowed
        )

    mixed = lax.map(one_item, jnp.arange(item_count, dtype=jnp.int32))
    mixed = jnp.moveaxis(mixed, 0, 1).reshape(tok_rows, item_count * heads_item * HEAD_SIZE)
    return lax.all_to_all(mixed, "head", split_axis=0, concat_axis=1, tiled=True)


def solution(mesh):
    placed = (P("ctx", "head"), P("ctx", "head"), P("ctx", "head"), P())
    return jax.shard_map(
        per_device, mesh=mesh, in_specs=placed, out_specs=P(("ctx", "head"), None), check_vma=False
    )
```

profile of v0, /device:TPU:128, one launch (start us, length us, event | category | flops | bytes accessed | tf_op | source)
XLA Modules:
  0.0 334.9 jit_solution(958149482969775816)
XLA Ops:
  4.7 155.5 %while.28 = (s32[]{:T(128)}, bf16[2,3072,256]{2,1,0:T(8,128)(2,1)S(1)}, bf16[2,192,256]{2,1,0:T(8,128)(2,1)S(1)}, s32[]{:T(128)}, s32[]{:T(128)}, /*index=5*/s32[]{:T(128)}, s32[]{:T(128)}, s32[]{:T(128)}) while((s32[]{:T(128)}, bf16[2,3072,256]{2,1,0:T(8,128)(2,1)S(1)}, bf16[2,192,256]{2,1,0:T(8,128)(2,1)S(1)}, s32[]{:T(128)}, s32[]{:T(128)}, ...), condition=%wide.region_1.0_spmd, body=%wide.region_0.0_spmd.sunk | while | flops 7 | bytes 1573051 | solution.py:50
  4.7 1.9 collective-permute-start
  6.7 8.4 %collective-permute-done = bf16[2,192,256]{2,1,0:T(8,128)(2,1)S(1)} collective-permute-done((bf16[2,192,256]{2,1,0:T(8,128)(2,1)S(1)}, bf16[2,192,256]{2,1,0:T(8,128)(2,1)S(1)}, u32[]{:S(2)}, u32[]{:S(2)}) %collective-permute-start) | collective-permute-done | bytes 196640 | tf_op jit(solution)/shard_map/while/body/eval_jaxpr/ppermute | solution.py:12
  15.1 1.9 collective-permute-start
  17.0 8.4 %collective-permute-done = bf16[2,192,256]{2,1,0:T(8,128)(2,1)S(1)} collective-permute-done((bf16[2,192,256]{2,1,0:T(8,128)(2,1)S(1)}, bf16[2,192,256]{2,1,0:T(8,128)(2,1)S(1)}, u32[]{:S(2)}, u32[]{:S(2)}) %collective-permute-start) | collective-permute-done | bytes 196640 | tf_op jit(solution)/shard_map/while/body/eval_jaxpr/ppermute | solution.py:12
  25.5 1.9 collective-permute-start
  27.4 8.4 %collective-permute-done = bf16[2,192,256]{2,1,0:T(8,128)(2,1)S(1)} collective-permute-done((bf16[2,192,256]{2,1,0:T(8,128)(2,1)S(1)}, bf16[2,192,256]{2,1,0:T(8,128)(2,1)S(1)}, u32[]{:S(2)}, u32[]{:S(2)}) %collective-permute-start) | collective-permute-done | bytes 196640 | tf_op jit(solution)/shard_map/while/body/eval_jaxpr/ppermute | solution.py:12
  35.8 1.9 collective-permute-start
  37.8 8.4 %collective-permute-done = bf16[2,192,256]{2,1,0:T(8,128)(2,1)S(1)} collective-permute-done((bf16[2,192,256]{2,1,0:T(8,128)(2,1)S(1)}, bf16[2,192,256]{2,1,0:T(8,128)(2,1)S(1)}, u32[]{:S(2)}, u32[]{:S(2)}) %collective-permute-start) | collective-permute-done | bytes 196640 | tf_op jit(solution)/shard_map/while/body/eval_jaxpr/ppermute | solution.py:12
  46.2 1.9 collective-permute-start
  48.1 8.4 %collective-permute-done = bf16[2,192,256]{2,1,0:T(8,128)(2,1)S(1)} collective-permute-done((bf16[2,192,256]{2,1,0:T(8,128)(2,1)S(1)}, bf16[2,192,256]{2,1,0:T(8,128)(2,1)S(1)}, u32[]{:S(2)}, u32[]{:S(2)}) %collective-permute-start) | collective-permute-done | bytes 196640 | tf_op jit(solution)/shard_map/while/body/eval_jaxpr/ppermute | solution.py:12
  56.6 1.9 collective-permute-start
  58.5 8.4 %collective-permute-done = bf16[2,192,256]{2,1,0:T(8,128)(2,1)S(1)} collective-permute-done((bf16[2,192,256]{2,1,0:T(8,128)(2,1)S(1)}, bf16[2,192,256]{2,1,0:T(8,128)(2,1)S(1)}, u32[]{:S(2)}, u32[]{:S(2)}) %collective-permute-start) | collective-permute-done | bytes 196640 | tf_op jit(solution)/shard_map/while/body/eval_jaxpr/ppermute | solution.py:12
  66.9 1.9 collective-permute-start
  68.9 8.4 %collective-permute-done = bf16[2,192,256]{2,1,0:T(8,128)(2,1)S(1)} collective-permute-done((bf16[2,192,256]{2,1,0:T(8,128)(2,1)S(1)}, bf16[2,192,256]{2,1,0:T(8,128)(2,1)S(1)}, u32[]{:S(2)}, u32[]{:S(2)}) %collective-permute-start) | collective-permute-done | bytes 196640 | tf_op jit(solution)/shard_map/while/body/eval_jaxpr/ppermute | solution.py:12
  77.3 1.9 collective-permute-start
  79.2 8.4 %collective-permute-done = bf16[2,192,256]{2,1,0:T(8,128)(2,1)S(1)} collective-permute-done((bf16[2,192,256]{2,1,0:T(8,128)(2,1)S(1)}, bf16[2,192,256]{2,1,0:T(8,128)(2,1)S(1)}, u32[]{:S(2)}, u32[]{:S(2)}) %collective-permute-start) | collective-permute-done | bytes 196640 | tf_op jit(solution)/shard_map/while/body/eval_jaxpr/ppermute | solution.py:12
  87.7 1.9 collective-permute-start
  89.6 8.4 %collective-permute-done = bf16[2,192,256]{2,1,0:T(8,128)(2,1)S(1)} collective-permute-done((bf16[2,192,256]{2,1,0:T(8,128)(2,1)S(1)}, bf16[2,192,256]{2,1,0:T(8,128)(2,1)S(1)}, u32[]{:S(2)}, u32[]{:S(2)}) %collective-permute-start) | collective-permute-done | bytes 196640 | tf_op jit(solution)/shard_map/while/body/eval_jaxpr/ppermute | solution.py:12
  98.0 1.9 collective-permute-start
  100.0 8.4 %collective-permute-done = bf16[2,192,256]{2,1,0:T(8,128)(2,1)S(1)} collective-permute-done((bf16[2,192,256]{2,1,0:T(8,128)(2,1)S(1)}, bf16[2,192,256]{2,1,0:T(8,128)(2,1)S(1)}, u32[]{:S(2)}, u32[]{:S(2)}) %collective-permute-start) | collective-permute-done | bytes 196640 | tf_op jit(solution)/shard_map/while/body/eval_jaxpr/ppermute | solution.py:12
  108.4 1.9 collective-permute-start
  110.4 8.4 %collective-permute-done = bf16[2,192,256]{2,1,0:T(8,128)(2,1)S(1)} collective-permute-done((bf16[2,192,256]{2,1,0:T(8,128)(2,1)S(1)}, bf16[2,192,256]{2,1,0:T(8,128)(2,1)S(1)}, u32[]{:S(2)}, u32[]{:S(2)}) %collective-permute-start) | collective-permute-done | bytes 196640 | tf_op jit(solution)/shard_map/while/body/eval_jaxpr/ppermute | solution.py:12
  120.7 8.4 %collective-permute-done = bf16[2,192,256]{2,1,0:T(8,128)(2,1)S(1)} collective-permute-done((bf16[2,192,256]{2,1,0:T(8,128)(2,1)S(1)}, bf16[2,192,256]{2,1,0:T(8,128)(2,1)S(1)}, u32[]{:S(2)}, u32[]{:S(2)}) %collective-permute-start) | collective-permute-done | bytes 196640 | tf_op jit(solution)/shard_map/while/body/eval_jaxpr/ppermute | solution.py:12
  131.1 8.4 %collective-permute-done = bf16[2,192,256]{2,1,0:T(8,128)(2,1)S(1)} collective-permute-done((bf16[2,192,256]{2,1,0:T(8,128)(2,1)S(1)}, bf16[2,192,256]{2,1,0:T(8,128)(2,1)S(1)}, u32[]{:S(2)}, u32[]{:S(2)}) %collective-permute-start) | collective-permute-done | bytes 196640 | tf_op jit(solution)/shard_map/while/body/eval_jaxpr/ppermute | solution.py:12
  141.5 8.4 %collective-permute-done = bf16[2,192,256]{2,1,0:T(8,128)(2,1)S(1)} collective-permute-done((bf16[2,192,256]{2,1,0:T(8,128)(2,1)S(1)}, bf16[2,192,256]{2,1,0:T(8,128)(2,1)S(1)}, u32[]{:S(2)}, u32[]{:S(2)}) %collective-permute-start) | collective-permute-done | bytes 196640 | tf_op jit(solution)/shard_map/while/body/eval_jaxpr/ppermute | solution.py:12
  151.8 8.4 %collective-permute-done = bf16[2,192,256]{2,1,0:T(8,128)(2,1)S(1)} collective-permute-done((bf16[2,192,256]{2,1,0:T(8,128)(2,1)S(1)}, bf16[2,192,256]{2,1,0:T(8,128)(2,1)S(1)}, u32[]{:S(2)}, u32[]{:S(2)}) %collective-permute-start) | collective-permute-done | bytes 196640 | tf_op jit(solution)/shard_map/while/body/eval_jaxpr/ppermute | solution.py:12
  160.3 3.1 copy.21
  163.3 3.9 %fusion.51 = (bf16[1,3072,256]{1,2,0:T(8,128)(2,1)}, bf16[1,3072,256]{1,2,0:T(8,128)(2,1)}) fusion(bf16[2,3072,256]{1,2,0:T(8,128)(2,1)} %copy.21), kind=kLoop, calls=%fused_computation.39 | loop fusion | bytes 6291456 | tf_op jit(solution)/shard_map/slice | solution.py:64
  168.6 143.1 %while.29 = (s32[]{:T(128)}, bf16[8,192,4,128]{3,1,2,0:T(8,128)(2,1)}, s32[8]{0:T(128)S(1)}, bf16[3072,2,128]{0,2,1:T(8,128)(2,1)}, bf16[3072,2,128]{0,2,1:T(8,1...) while((s32[]{:T(128)}, ...), condition=%wide.region_8.9_spmd.clone, body=%wide.region_5.8_spmd.clone.sunk | while | flops 1224084480 | bytes 13599102 | solution.py:73
  174.0 7.8 %fusion.61 = (f32[4,192]{1,0:T(4,128)S(1)}, bf16[4,192,3072]{2,1,0:T(8,128)(2,1)}) fusion(pred[192,3072]{1,0:T(8,128)(4,1)S(1)} %compare_and_fusion.2, bf16[3072,2,128]{0,2,1:T(8,128)(2,1)} %get-tuple-element.393, s32[]{:T(128)S(6)} %select_n.75, bf16[1,192,4,128]{3,2,0,1:T(4,128)(2,1)S(1)} %constant_dynamic-slice_fusion.2), kind=kOutput, calls=%fused_computation.38.clone.1 | convolution fusion | flops 618138624 | bytes 6884356 | tf_op jit(solution)/shard_map/while/body/eval_jaxpr/sub | solution.py:21
  181.8 4.6 %fusion.62 = bf16[8,192,4,128]{3,1,2,0:T(8,128)(2,1)} fusion(bf16[8,192,4,128]{3,1,2,0:T(8,128)(2,1)} %get-tuple-element.374, s32[]{:T(128)} %get-tuple-element.373, bf16[4,192,3072]{2,1,0:T(8,128)(2,1)} %get-tuple-element.331, bf16[3072,2,128]{0,2,1:T(8,128)(2,1)} %get-tuple-element.392, s32[]{:T(128)S(6)} %select_n.75, f32[192,4]{0,1:T(4,128)S(1)} %bitcast.94), kind=kOutput, calls=%fused_computation.17.clone.1 | convolution fusion | flops 604176384 | bytes 5705220 | tf_op jit(solution)/shard_map/while/body/eval_jaxpr/hqk,kd->qhd/dot_general | solution.py:24
  191.9 7.8 %fusion.61 = (f32[4,192]{1,0:T(4,128)S(1)}, bf16[4,192,3072]{2,1,0:T(8,128)(2,1)}) fusion(pred[192,3072]{1,0:T(8,128)(4,1)S(1)} %compare_and_fusion.2, bf16[3072,2,128]{0,2,1:T(8,128)(2,1)} %get-tuple-element.393, s32[]{:T(128)S(6)} %select_n.75, bf16[1,192,4,128]{3,2,0,1:T(4,128)(2,1)S(1)} %constant_dynamic-slice_fusion.2), kind=kOutput, calls=%fused_computation.38.clone.1 | convolution fusion | flops 618138624 | bytes 6884356 | tf_op jit(solution)/shard_map/while/body/eval_jaxpr/sub | solution.py:21
  199.7 4.6 %fusion.62 = bf16[8,192,4,128]{3,1,2,0:T(8,128)(2,1)} fusion(bf16[8,192,4,128]{3,1,2,0:T(8,128)(2,1)} %get-tuple-element.374, s32[]{:T(128)} %get-tuple-element.373, bf16[4,192,3072]{2,1,0:T(8,128)(2,1)} %get-tuple-element.331, bf16[3072,2,128]{0,2,1:T(8,128)(2,1)} %get-tuple-element.392, s32[]{:T(128)S(6)} %select_n.75, f32[192,4]{0,1:T(4,128)S(1)} %bitcast.94), kind=kOutput, calls=%fused_computation.17.clone.1 | convolution fusion | flops 604176384 | bytes 5705220 | tf_op jit(solution)/shard_map/while/body/eval_jaxpr/hqk,kd->qhd/dot_general | solution.py:24
  209.8 7.8 %fusion.61 = (f32[4,192]{1,0:T(4,128)S(1)}, bf16[4,192,3072]{2,1,0:T(8,128)(2,1)}) fusion(pred[192,3072]{1,0:T(8,128)(4,1)S(1)} %compare_and_fusion.2, bf16[3072,2,128]{0,2,1:T(8,128)(2,1)} %get-tuple-element.393, s32[]{:T(128)S(6)} %select_n.75, bf16[1,192,4,128]{3,2,0,1:T(4,128)(2,1)S(1)} %constant_dynamic-slice_fusion.2), kind=kOutput, calls=%fused_computation.38.clone.1 | convolution fusion | flops 618138624 | bytes 6884356 | tf_op jit(solution)/shard_map/while/body/eval_jaxpr/sub | solution.py:21
  217.6 4.6 %fusion.62 = bf16[8,192,4,128]{3,1,2,0:T(8,128)(2,1)} fusion(bf16[8,192,4,128]{3,1,2,0:T(8,128)(2,1)} %get-tuple-element.374, s32[]{:T(128)} %get-tuple-element.373, bf16[4,192,3072]{2,1,0:T(8,128)(2,1)} %get-tuple-element.331, bf16[3072,2,128]{0,2,1:T(8,128)(2,1)} %get-tuple-element.392, s32[]{:T(128)S(6)} %select_n.75, f32[192,4]{0,1:T(4,128)S(1)} %bitcast.94), kind=kOutput, calls=%fused_computation.17.clone.1 | convolution fusion | flops 604176384 | bytes 5705220 | tf_op jit(solution)/shard_map/while/body/eval_jaxpr/hqk,kd->qhd/dot_general | solution.py:24
  227.7 7.8 %fusion.61 = (f32[4,192]{1,0:T(4,128)S(1)}, bf16[4,192,3072]{2,1,0:T(8,128)(2,1)}) fusion(pred[192,3072]{1,0:T(8,128)(4,1)S(1)} %compare_and_fusion.2, bf16[3072,2,128]{0,2,1:T(8,128)(2,1)} %get-tuple-element.393, s32[]{:T(128)S(6)} %select_n.75, bf16[1,192,4,128]{3,2,0,1:T(4,128)(2,1)S(1)} %constant_dynamic-slice_fusion.2), kind=kOutput, calls=%fused_computation.38.clone.1 | convolution fusion | flops 618138624 | bytes 6884356 | tf_op jit(solution)/shard_map/while/body/eval_jaxpr/sub | solution.py:21
  235.5 4.6 %fusion.62 = bf16[8,192,4,128]{3,1,2,0:T(8,128)(2,1)} fusion(bf16[8,192,4,128]{3,1,2,0:T(8,128)(2,1)} %get-tuple-element.374, s32[]{:T(128)} %get-tuple-element.373, bf16[4,192,3072]{2,1,0:T(8,128)(2,1)} %get-tuple-element.331, bf16[3072,2,128]{0,2,1:T(8,128)(2,1)} %get-tuple-element.392, s32[]{:T(128)S(6)} %select_n.75, f32[192,4]{0,1:T(4,128)S(1)} %bitcast.94), kind=kOutput, calls=%fused_computation.17.clone.1 | convolution fusion | flops 604176384 | bytes 5705220 | tf_op jit(solution)/shard_map/while/body/eval_jaxpr/hqk,kd->qhd/dot_general | solution.py:24
  245.6 7.8 %fusion.61 = (f32[4,192]{1,0:T(4,128)S(1)}, bf16[4,192,3072]{2,1,0:T(8,128)(2,1)}) fusion(pred[192,3072]{1,0:T(8,128)(4,1)S(1)} %compare_and_fusion.2, bf16[3072,2,128]{0,2,1:T(8,128)(2,1)} %get-tuple-element.393, s32[]{:T(128)S(6)} %select_n.75, bf16[1,192,4,128]{3,2,0,1:T(4,128)(2,1)S(1)} %constant_dynamic-slice_fusion.2), kind=kOutput, calls=%fused_computation.38.clone.1 | convolution fusion | flops 618138624 | bytes 6884356 | tf_op jit(solution)/shard_map/while/body/eval_jaxpr/sub | solution.py:21
  253.3 4.6 %fusion.62 = bf16[8,192,4,128]{3,1,2,0:T(8,128)(2,1)} fusion(bf16[8,192,4,128]{3,1,2,0:T(8,128)(2,1)} %get-tuple-element.374, s32[]{:T(128)} %get-tuple-element.373, bf16[4,192,3072]{2,1,0:T(8,128)(2,1)} %get-tuple-element.331, bf16[3072,2,128]{0,2,1:T(8,128)(2,1)} %get-tuple-element.392, s32[]{:T(128)S(6)} %select_n.75, f32[192,4]{0,1:T(4,128)S(1)} %bitcast.94), kind=kOutput, calls=%fused_computation.17.clone.1 | convolution fusion | flops 604176384 | bytes 5705220 | tf_op jit(solution)/shard_map/while/body/eval_jaxpr/hqk,kd->qhd/dot_general | solution.py:24
  263.4 7.8 %fusion.61 = (f32[4,192]{1,0:T(4,128)S(1)}, bf16[4,192,3072]{2,1,0:T(8,128)(2,1)}) fusion(pred[192,3072]{1,0:T(8,128)(4,1)S(1)} %compare_and_fusion.2, bf16[3072,2,128]{0,2,1:T(8,128)(2,1)} %get-tuple-element.393, s32[]{:T(128)S(6)} %select_n.75, bf16[1,192,4,128]{3,2,0,1:T(4,128)(2,1)S(1)} %constant_dynamic-slice_fusion.2), kind=kOutput, calls=%fused_computation.38.clone.1 | convolution fusion | flops 618138624 | bytes 6884356 | tf_op jit(solution)/shard_map/while/body/eval_jaxpr/sub | solution.py:21
  271.2 4.6 %fusion.62 = bf16[8,192,4,128]{3,1,2,0:T(8,128)(2,1)} fusion(bf16[8,192,4,128]{3,1,2,0:T(8,128)(2,1)} %get-tuple-element.374, s32[]{:T(128)} %get-tuple-element.373, bf16[4,192,3072]{2,1,0:T(8,128)(2,1)} %get-tuple-element.331, bf16[3072,2,128]{0,2,1:T(8,128)(2,1)} %get-tuple-element.392, s32[]{:T(128)S(6)} %select_n.75, f32[192,4]{0,1:T(4,128)S(1)} %bitcast.94), kind=kOutput, calls=%fused_computation.17.clone.1 | convolution fusion | flops 604176384 | bytes 5705220 | tf_op jit(solution)/shard_map/while/body/eval_jaxpr/hqk,kd->qhd/dot_general | solution.py:24
  281.3 7.8 %fusion.61 = (f32[4,192]{1,0:T(4,128)S(1)}, bf16[4,192,3072]{2,1,0:T(8,128)(2,1)}) fusion(pred[192,3072]{1,0:T(8,128)(4,1)S(1)} %compare_and_fusion.2, bf16[3072,2,128]{0,2,1:T(8,128)(2,1)} %get-tuple-element.393, s32[]{:T(128)S(6)} %select_n.75, bf16[1,192,4,128]{3,2,0,1:T(4,128)(2,1)S(1)} %constant_dynamic-slice_fusion.2), kind=kOutput, calls=%fused_computation.38.clone.1 | convolution fusion | flops 618138624 | bytes 6884356 | tf_op jit(solution)/shard_map/while/body/eval_jaxpr/sub | solution.py:21
  289.1 4.6 %fusion.62 = bf16[8,192,4,128]{3,1,2,0:T(8,128)(2,1)} fusion(bf16[8,192,4,128]{3,1,2,0:T(8,128)(2,1)} %get-tuple-element.374, s32[]{:T(128)} %get-tuple-element.373, bf16[4,192,3072]{2,1,0:T(8,128)(2,1)} %get-tuple-element.331, bf16[3072,2,128]{0,2,1:T(8,128)(2,1)} %get-tuple-element.392, s32[]{:T(128)S(6)} %select_n.75, f32[192,4]{0,1:T(4,128)S(1)} %bitcast.94), kind=kOutput, calls=%fused_computation.17.clone.1 | convolution fusion | flops 604176384 | bytes 5705220 | tf_op jit(solution)/shard_map/while/body/eval_jaxpr/hqk,kd->qhd/dot_general | solution.py:24
  299.2 7.8 %fusion.61 = (f32[4,192]{1,0:T(4,128)S(1)}, bf16[4,192,3072]{2,1,0:T(8,128)(2,1)}) fusion(pred[192,3072]{1,0:T(8,128)(4,1)S(1)} %compare_and_fusion.2, bf16[3072,2,128]{0,2,1:T(8,128)(2,1)} %get-tuple-element.393, s32[]{:T(128)S(6)} %select_n.75, bf16[1,192,4,128]{3,2,0,1:T(4,128)(2,1)S(1)} %constant_dynamic-slice_fusion.2), kind=kOutput, calls=%fused_computation.38.clone.1 | convolution fusion | flops 618138624 | bytes 6884356 | tf_op jit(solution)/shard_map/while/body/eval_jaxpr/sub | solution.py:21
  307.0 4.6 %fusion.62 = bf16[8,192,4,128]{3,1,2,0:T(8,128)(2,1)} fusion(bf16[8,192,4,128]{3,1,2,0:T(8,128)(2,1)} %get-tuple-element.374, s32[]{:T(128)} %get-tuple-element.373, bf16[4,192,3072]{2,1,0:T(8,128)(2,1)} %get-tuple-element.331, bf16[3072,2,128]{0,2,1:T(8,128)(2,1)} %get-tuple-element.392, s32[]{:T(128)S(6)} %select_n.75, f32[192,4]{0,1:T(4,128)S(1)} %bitcast.94), kind=kOutput, calls=%fused_computation.17.clone.1 | convolution fusion | flops 604176384 | bytes 5705220 | tf_op jit(solution)/shard_map/while/body/eval_jaxpr/hqk,kd->qhd/dot_general | solution.py:24
  311.6 2.6 copy.27
  315.5 18.2 %all_to_all.19 = bf16[4,48,4096]{2,1,0:T(8,128)(2,1)S(1)} all-to-all(bf16[4,48,4096]{2,1,0:T(8,128)(2,1)S(1)} %all_to_all.14), channel_id=1, replica_groups=mesh['ctx'=64,'head'=4] {'head'}, dimensions={0} | all-to-all | bytes 3145728 | tf_op jit(solution)/shard_map/all_to_all | solution.py:75
  (77 shorter events, 26.8 us)
Async XLA Ops:
  4.7 10.3 %collective-permute-start = (bf16[2,192,256]{2,1,0:T(8,128)(2,1)S(1)}, bf16[2,192,256]{2,1,0:T(8,128)(2,1)S(1)}, u32[]{:S(2)}, u32[]{:S(2)}) collective-permute-start(bf16[2,192,256]{2,1,0:T(8,128)(2,1)S(1)} %get-tuple-element.343), channel_id=1, source_target_pairs={{0,4},{4,8},{8,12},{12,16},{16,20},{20,24},{24,28},{28,32},{32,36}... | collective-permute-start | bytes 589832 | tf_op jit(solution)/shard_map/while/body/eval_jaxpr/ppermute | solution.py:12
  15.1 10.3 %collective-permute-start = (bf16[2,192,256]{2,1,0:T(8,128)(2,1)S(1)}, bf16[2,192,256]{2,1,0:T(8,128)(2,1)S(1)}, u32[]{:S(2)}, u32[]{:S(2)}) collective-permute-start(bf16[2,192,256]{2,1,0:T(8,128)(2,1)S(1)} %get-tuple-element.343), channel_id=1, source_target_pairs={{0,4},{4,8},{8,12},{12,16},{16,20},{20,24},{24,28},{28,32},{32,36}... | collective-permute-start | bytes 589832 | tf_op jit(solution)/shard_map/while/body/eval_jaxpr/ppermute | solution.py:12
  25.5 10.3 %collective-permute-start = (bf16[2,192,256]{2,1,0:T(8,128)(2,1)S(1)}, bf16[2,192,256]{2,1,0:T(8,128)(2,1)S(1)}, u32[]{:S(2)}, u32[]{:S(2)}) collective-permute-start(bf16[2,192,256]{2,1,0:T(8,128)(2,1)S(1)} %get-tuple-element.343), channel_id=1, source_target_pairs={{0,4},{4,8},{8,12},{12,16},{16,20},{20,24},{24,28},{28,32},{32,36}... | collective-permute-start | bytes 589832 | tf_op jit(solution)/shard_map/while/body/eval_jaxpr/ppermute | solution.py:12
  35.8 10.3 %collective-permute-start = (bf16[2,192,256]{2,1,0:T(8,128)(2,1)S(1)}, bf16[2,192,256]{2,1,0:T(8,128)(2,1)S(1)}, u32[]{:S(2)}, u32[]{:S(2)}) collective-permute-start(bf16[2,192,256]{2,1,0:T(8,128)(2,1)S(1)} %get-tuple-element.343), channel_id=1, source_target_pairs={{0,4},{4,8},{8,12},{12,16},{16,20},{20,24},{24,28},{28,32},{32,36}... | collective-permute-start | bytes 589832 | tf_op jit(solution)/shard_map/while/body/eval_jaxpr/ppermute | solution.py:12
  46.2 10.3 %collective-permute-start = (bf16[2,192,256]{2,1,0:T(8,128)(2,1)S(1)}, bf16[2,192,256]{2,1,0:T(8,128)(2,1)S(1)}, u32[]{:S(2)}, u32[]{:S(2)}) collective-permute-start(bf16[2,192,256]{2,1,0:T(8,128)(2,1)S(1)} %get-tuple-element.343), channel_id=1, source_target_pairs={{0,4},{4,8},{8,12},{12,16},{16,20},{20,24},{24,28},{28,32},{32,36}... | collective-permute-start | bytes 589832 | tf_op jit(solution)/shard_map/while/body/eval_jaxpr/ppermute | solution.py:12
  56.6 10.3 %collective-permute-start = (bf16[2,192,256]{2,1,0:T(8,128)(2,1)S(1)}, bf16[2,192,256]{2,1,0:T(8,128)(2,1)S(1)}, u32[]{:S(2)}, u32[]{:S(2)}) collective-permute-start(bf16[2,192,256]{2,1,0:T(8,128)(2,1)S(1)} %get-tuple-element.343), channel_id=1, source_target_pairs={{0,4},{4,8},{8,12},{12,16},{16,20},{20,24},{24,28},{28,32},{32,36}... | collective-permute-start | bytes 589832 | tf_op jit(solution)/shard_map/while/body/eval_jaxpr/ppermute | solution.py:12
  66.9 10.3 %collective-permute-start = (bf16[2,192,256]{2,1,0:T(8,128)(2,1)S(1)}, bf16[2,192,256]{2,1,0:T(8,128)(2,1)S(1)}, u32[]{:S(2)}, u32[]{:S(2)}) collective-permute-start(bf16[2,192,256]{2,1,0:T(8,128)(2,1)S(1)} %get-tuple-element.343), channel_id=1, source_target_pairs={{0,4},{4,8},{8,12},{12,16},{16,20},{20,24},{24,28},{28,32},{32,36}... | collective-permute-start | bytes 589832 | tf_op jit(solution)/shard_map/while/body/eval_jaxpr/ppermute | solution.py:12
  77.3 10.3 %collective-permute-start = (bf16[2,192,256]{2,1,0:T(8,128)(2,1)S(1)}, bf16[2,192,256]{2,1,0:T(8,128)(2,1)S(1)}, u32[]{:S(2)}, u32[]{:S(2)}) collective-permute-start(bf16[2,192,256]{2,1,0:T(8,128)(2,1)S(1)} %get-tuple-element.343), channel_id=1, source_target_pairs={{0,4},{4,8},{8,12},{12,16},{16,20},{20,24},{24,28},{28,32},{32,36}... | collective-permute-start | bytes 589832 | tf_op jit(solution)/shard_map/while/body/eval_jaxpr/ppermute | solution.py:12
  87.7 10.3 %collective-permute-start = (bf16[2,192,256]{2,1,0:T(8,128)(2,1)S(1)}, bf16[2,192,256]{2,1,0:T(8,128)(2,1)S(1)}, u32[]{:S(2)}, u32[]{:S(2)}) collective-permute-start(bf16[2,192,256]{2,1,0:T(8,128)(2,1)S(1)} %get-tuple-element.343), channel_id=1, source_target_pairs={{0,4},{4,8},{8,12},{12,16},{16,20},{20,24},{24,28},{28,32},{32,36}... | collective-permute-start | bytes 589832 | tf_op jit(solution)/shard_map/while/body/eval_jaxpr/ppermute | solution.py:12
  98.0 10.3 %collective-permute-start = (bf16[2,192,256]{2,1,0:T(8,128)(2,1)S(1)}, bf16[2,192,256]{2,1,0:T(8,128)(2,1)S(1)}, u32[]{:S(2)}, u32[]{:S(2)}) collective-permute-start(bf16[2,192,256]{2,1,0:T(8,128)(2,1)S(1)} %get-tuple-element.343), channel_id=1, source_target_pairs={{0,4},{4,8},{8,12},{12,16},{16,20},{20,24},{24,28},{28,32},{32,36}... | collective-permute-start | bytes 589832 | tf_op jit(solution)/shard_map/while/body/eval_jaxpr/ppermute | solution.py:12
  108.4 10.3 %collective-permute-start = (bf16[2,192,256]{2,1,0:T(8,128)(2,1)S(1)}, bf16[2,192,256]{2,1,0:T(8,128)(2,1)S(1)}, u32[]{:S(2)}, u32[]{:S(2)}) collective-permute-start(bf16[2,192,256]{2,1,0:T(8,128)(2,1)S(1)} %get-tuple-element.343), channel_id=1, source_target_pairs={{0,4},{4,8},{8,12},{12,16},{16,20},{20,24},{24,28},{28,32},{32,36}... | collective-permute-start | bytes 589832 | tf_op jit(solution)/shard_map/while/body/eval_jaxpr/ppermute | solution.py:12
  118.8 10.3 %collective-permute-start = (bf16[2,192,256]{2,1,0:T(8,128)(2,1)S(1)}, bf16[2,192,256]{2,1,0:T(8,128)(2,1)S(1)}, u32[]{:S(2)}, u32[]{:S(2)}) collective-permute-start(bf16[2,192,256]{2,1,0:T(8,128)(2,1)S(1)} %get-tuple-element.343), channel_id=1, source_target_pairs={{0,4},{4,8},{8,12},{12,16},{16,20},{20,24},{24,28},{28,32},{32,36}... | collective-permute-start | bytes 589832 | tf_op jit(solution)/shard_map/while/body/eval_jaxpr/ppermute | solution.py:12
  129.2 10.3 %collective-permute-start = (bf16[2,192,256]{2,1,0:T(8,128)(2,1)S(1)}, bf16[2,192,256]{2,1,0:T(8,128)(2,1)S(1)}, u32[]{:S(2)}, u32[]{:S(2)}) collective-permute-start(bf16[2,192,256]{2,1,0:T(8,128)(2,1)S(1)} %get-tuple-element.343), channel_id=1, source_target_pairs={{0,4},{4,8},{8,12},{12,16},{16,20},{20,24},{24,28},{28,32},{32,36}... | collective-permute-start | bytes 589832 | tf_op jit(solution)/shard_map/while/body/eval_jaxpr/ppermute | solution.py:12
  139.5 10.3 %collective-permute-start = (bf16[2,192,256]{2,1,0:T(8,128)(2,1)S(1)}, bf16[2,192,256]{2,1,0:T(8,128)(2,1)S(1)}, u32[]{:S(2)}, u32[]{:S(2)}) collective-permute-start(bf16[2,192,256]{2,1,0:T(8,128)(2,1)S(1)} %get-tuple-element.343), channel_id=1, source_target_pairs={{0,4},{4,8},{8,12},{12,16},{16,20},{20,24},{24,28},{28,32},{32,36}... | collective-permute-start | bytes 589832 | tf_op jit(solution)/shard_map/while/body/eval_jaxpr/ppermute | solution.py:12
  149.9 10.3 %collective-permute-start = (bf16[2,192,256]{2,1,0:T(8,128)(2,1)S(1)}, bf16[2,192,256]{2,1,0:T(8,128)(2,1)S(1)}, u32[]{:S(2)}, u32[]{:S(2)}) collective-permute-start(bf16[2,192,256]{2,1,0:T(8,128)(2,1)S(1)} %get-tuple-element.343), channel_id=1, source_target_pairs={{0,4},{4,8},{8,12},{12,16},{16,20},{20,24},{24,28},{28,32},{32,36}... | collective-permute-start | bytes 589832 | tf_op jit(solution)/shard_map/while/body/eval_jaxpr/ppermute | solution.py:12
  163.3 4.1 %copy-start = (bf16[192,4096]{1,0:T(8,128)(2,1)S(1)}, bf16[192,4096]{1,0:T(8,128)(2,1)}, u32[]{:S(2)}) copy-start(bf16[192,4096]{1,0:T(8,128)(2,1)} %param.8) | copy-start | bytes 4718596
  167.2 1.4 copy-start.1
where the time goes:
time: 336 us; the launch traced here: 335 us
  waiting for transfers between devices  126 us (38%)
  matrix products  99.5 us (30%)
  loops' own time  34.1 us (10%)
  starting transfers between devices  28.8 us (9%)
  local copies, waits for them, and re-layouts  20.6 us (6%)
  blocking collectives  18.2 us (5%)
  other arithmetic  8.1 us (2%)
    ppermute x15, waiting for transfers between devices, passed_along(): lax.ppermute(value, axis, [(source, source + steps) for source in range(l...  126 us
    sub x8, matrix products, attend_group(): probs = jnp.where(allowed[None], jnp.exp(scores - highest), 0.0)  62.3 us
    dot_general x8, matrix products, attend_group(): jnp.einsum('hqk,kd->qhd', rounded, value_part, preferred_element_type=jnp...  37.2 us
    another operation x1, loops' own time, per_device(): mixed = lax.map(one_item, jnp.arange(item_count, dtype=jnp.int32))  33.4 us
    ppermute x15, starting transfers between devices, passed_along(): lax.ppermute(value, axis, [(source, source + steps) for source in range(l...  28.8 us
    all_to_all x1, blocking collectives, per_device(): lax.all_to_all(mixed, 'head', split_axis=0, concat_axis=1, tiled=True)  18.2 us
  transfers between devices with their start and end apart: 15, of which 15 were waited for; matrix products, arithmetic and copies ran while one was open for 0% of the time, Pallas kernels for 0%

commit v1 on v0

--- a/solution.py
+++ b/solution.py
@@ -72,7 +72,15 @@
 
     mixed = lax.map(one_item, jnp.arange(item_count, dtype=jnp.int32))
     mixed = jnp.moveaxis(mixed, 0, 1).reshape(tok_rows, item_count * heads_item * HEAD_SIZE)
-    return lax.all_to_all(mixed, "head", split_axis=0, concat_axis=1, tiled=True)
+
+    def advance_strings_on(tile_in, axis_id):
+        u1 = jnp.concatenate(
+            lax.all_to_all(jnp.stack(jnp.split(tile_in, lax.axis_size(axis_id), 0)), axis_id, 0, 0),
+            1,
+        )
+        return u1
+
+    return advance_strings_on(mixed, "head")
 
 
 def solution(mesh):

time: 336 us -> 336 us (level)
  no operation moved by 1% of the time
where the time goes in v1:
time: 336 us; the launch traced here: 335 us
  waiting for transfers between devices  126 us (38%)
  matrix products  99.5 us (30%)
  loops' own time  34.1 us (10%)
  starting transfers between devices  28.8 us (9%)
  local copies, waits for them, and re-layouts  19.9 us (6%)
  blocking collectives  18.2 us (5%)
  other arithmetic  8.3 us (2%)
    ppermute x15, waiting for transfers between devices, passed_along(): lax.ppermute(value, axis, [(source, source + steps) for source in range(l...  126 us
    sub x8, matrix products, attend_group(): probs = jnp.where(allowed[None], jnp.exp(scores - highest), 0.0)  62.4 us
    dot_general x8, matrix products, attend_group(): jnp.einsum('hqk,kd->qhd', rounded, value_part, preferred_element_type=jnp...  37.2 us
    another operation x1, loops' own time, per_device(): mixed = lax.map(one_item, jnp.arange(item_count, dtype=jnp.int32))  33.4 us
    ppermute x15, starting transfers between devices, passed_along(): lax.ppermute(value, axis, [(source, source + steps) for source in range(l...  28.8 us
    all_to_all x1, blocking collectives, advance_strings_on(): lax.all_to_all(jnp.stack(jnp.split(tile_in, lax.axis_size(axis_id), 0)),...  18.2 us
  transfers between devices with their start and end apart: 15, of which 15 were waited for; matrix products, arithmetic and copies ran while one was open for 0% of the time, Pallas kernels for 0%

profile of v1, /device:TPU:128, one launch (start us, length us, event | category | flops | bytes accessed | tf_op | source)
XLA Modules:
  0.0 334.6 jit_solution(12332290125141505312)
XLA Ops:
  4.7 155.5 %while.28 = (s32[]{:T(128)}, bf16[2,3072,256]{2,1,0:T(8,128)(2,1)S(1)}, bf16[2,192,256]{2,1,0:T(8,128)(2,1)S(1)}, s32[]{:T(128)}, s32[]{:T(128)}, /*index=5*/s32[]{:T(128)}, s32[]{:T(128)}, s32[]{:T(128)}) while((s32[]{:T(128)}, bf16[2,3072,256]{2,1,0:T(8,128)(2,1)S(1)}, bf16[2,192,256]{2,1,0:T(8,128)(2,1)S(1)}, s32[]{:T(128)}, s32[]{:T(128)}, ...), condition=%wide.region_1.0_spmd, body=%wide.region_0.0_spmd.sunk | while | flops 7 | bytes 1573051 | solution.py:50
  4.7 1.9 collective-permute-start
  6.7 8.4 %collective-permute-done = bf16[2,192,256]{2,1,0:T(8,128)(2,1)S(1)} collective-permute-done((bf16[2,192,256]{2,1,0:T(8,128)(2,1)S(1)}, bf16[2,192,256]{2,1,0:T(8,128)(2,1)S(1)}, u32[]{:S(2)}, u32[]{:S(2)}) %collective-permute-start) | collective-permute-done | bytes 196640 | tf_op jit(solution)/shard_map/while/body/eval_jaxpr/ppermute | solution.py:12
  15.1 1.9 collective-permute-start
  17.0 8.4 %collective-permute-done = bf16[2,192,256]{2,1,0:T(8,128)(2,1)S(1)} collective-permute-done((bf16[2,192,256]{2,1,0:T(8,128)(2,1)S(1)}, bf16[2,192,256]{2,1,0:T(8,128)(2,1)S(1)}, u32[]{:S(2)}, u32[]{:S(2)}) %collective-permute-start) | collective-permute-done | bytes 196640 | tf_op jit(solution)/shard_map/while/body/eval_jaxpr/ppermute | solution.py:12
  25.5 1.9 collective-permute-start
  27.4 8.4 %collective-permute-done = bf16[2,192,256]{2,1,0:T(8,128)(2,1)S(1)} collective-permute-done((bf16[2,192,256]{2,1,0:T(8,128)(2,1)S(1)}, bf16[2,192,256]{2,1,0:T(8,128)(2,1)S(1)}, u32[]{:S(2)}, u32[]{:S(2)}) %collective-permute-start) | collective-permute-done | bytes 196640 | tf_op jit(solution)/shard_map/while/body/eval_jaxpr/ppermute | solution.py:12
  35.8 1.9 collective-permute-start
  37.8 8.4 %collective-permute-done = bf16[2,192,256]{2,1,0:T(8,128)(2,1)S(1)} collective-permute-done((bf16[2,192,256]{2,1,0:T(8,128)(2,1)S(1)}, bf16[2,192,256]{2,1,0:T(8,128)(2,1)S(1)}, u32[]{:S(2)}, u32[]{:S(2)}) %collective-permute-start) | collective-permute-done | bytes 196640 | tf_op jit(solution)/shard_map/while/body/eval_jaxpr/ppermute | solution.py:12
  46.2 1.9 collective-permute-start
  48.1 8.4 %collective-permute-done = bf16[2,192,256]{2,1,0:T(8,128)(2,1)S(1)} collective-permute-done((bf16[2,192,256]{2,1,0:T(8,128)(2,1)S(1)}, bf16[2,192,256]{2,1,0:T(8,128)(2,1)S(1)}, u32[]{:S(2)}, u32[]{:S(2)}) %collective-permute-start) | collective-permute-done | bytes 196640 | tf_op jit(solution)/shard_map/while/body/eval_jaxpr/ppermute | solution.py:12
  56.6 1.9 collective-permute-start
  58.5 8.4 %collective-permute-done = bf16[2,192,256]{2,1,0:T(8,128)(2,1)S(1)} collective-permute-done((bf16[2,192,256]{2,1,0:T(8,128)(2,1)S(1)}, bf16[2,192,256]{2,1,0:T(8,128)(2,1)S(1)}, u32[]{:S(2)}, u32[]{:S(2)}) %collective-permute-start) | collective-permute-done | bytes 196640 | tf_op jit(solution)/shard_map/while/body/eval_jaxpr/ppermute | solution.py:12
  66.9 1.9 collective-permute-start
  68.9 8.4 %collective-permute-done = bf16[2,192,256]{2,1,0:T(8,128)(2,1)S(1)} collective-permute-done((bf16[2,192,256]{2,1,0:T(8,128)(2,1)S(1)}, bf16[2,192,256]{2,1,0:T(8,128)(2,1)S(1)}, u32[]{:S(2)}, u32[]{:S(2)}) %collective-permute-start) | collective-permute-done | bytes 196640 | tf_op jit(solution)/shard_map/while/body/eval_jaxpr/ppermute | solution.py:12
  77.3 1.9 collective-permute-start
  79.2 8.4 %collective-permute-done = bf16[2,192,256]{2,1,0:T(8,128)(2,1)S(1)} collective-permute-done((bf16[2,192,256]{2,1,0:T(8,128)(2,1)S(1)}, bf16[2,192,256]{2,1,0:T(8,128)(2,1)S(1)}, u32[]{:S(2)}, u32[]{:S(2)}) %collective-permute-start) | collective-permute-done | bytes 196640 | tf_op jit(solution)/shard_map/while/body/eval_jaxpr/ppermute | solution.py:12
  87.7 1.9 collective-permute-start
  89.6 8.4 %collective-permute-done = bf16[2,192,256]{2,1,0:T(8,128)(2,1)S(1)} collective-permute-done((bf16[2,192,256]{2,1,0:T(8,128)(2,1)S(1)}, bf16[2,192,256]{2,1,0:T(8,128)(2,1)S(1)}, u32[]{:S(2)}, u32[]{:S(2)}) %collective-permute-start) | collective-permute-done | bytes 196640 | tf_op jit(solution)/shard_map/while/body/eval_jaxpr/ppermute | solution.py:12
  98.0 1.9 collective-permute-start
  100.0 8.4 %collective-permute-done = bf16[2,192,256]{2,1,0:T(8,128)(2,1)S(1)} collective-permute-done((bf16[2,192,256]{2,1,0:T(8,128)(2,1)S(1)}, bf16[2,192,256]{2,1,0:T(8,128)(2,1)S(1)}, u32[]{:S(2)}, u32[]{:S(2)}) %collective-permute-start) | collective-permute-done | bytes 196640 | tf_op jit(solution)/shard_map/while/body/eval_jaxpr/ppermute | solution.py:12
  108.4 1.9 collective-permute-start
  110.4 8.4 %collective-permute-done = bf16[2,192,256]{2,1,0:T(8,128)(2,1)S(1)} collective-permute-done((bf16[2,192,256]{2,1,0:T(8,128)(2,1)S(1)}, bf16[2,192,256]{2,1,0:T(8,128)(2,1)S(1)}, u32[]{:S(2)}, u32[]{:S(2)}) %collective-permute-start) | collective-permute-done | bytes 196640 | tf_op jit(solution)/shard_map/while/body/eval_jaxpr/ppermute | solution.py:12
  118.8 1.9 collective-permute-start
  120.7 8.4 %collective-permute-done = bf16[2,192,256]{2,1,0:T(8,128)(2,1)S(1)} collective-permute-done((bf16[2,192,256]{2,1,0:T(8,128)(2,1)S(1)}, bf16[2,192,256]{2,1,0:T(8,128)(2,1)S(1)}, u32[]{:S(2)}, u32[]{:S(2)}) %collective-permute-start) | collective-permute-done | bytes 196640 | tf_op jit(solution)/shard_map/while/body/eval_jaxpr/ppermute | solution.py:12
  131.1 8.4 %collective-permute-done = bf16[2,192,256]{2,1,0:T(8,128)(2,1)S(1)} collective-permute-done((bf16[2,192,256]{2,1,0:T(8,128)(2,1)S(1)}, bf16[2,192,256]{2,1,0:T(8,128)(2,1)S(1)}, u32[]{:S(2)}, u32[]{:S(2)}) %collective-permute-start) | collective-permute-done | bytes 196640 | tf_op jit(solution)/shard_map/while/body/eval_jaxpr/ppermute | solution.py:12
  141.5 8.4 %collective-permute-done = bf16[2,192,256]{2,1,0:T(8,128)(2,1)S(1)} collective-permute-done((bf16[2,192,256]{2,1,0:T(8,128)(2,1)S(1)}, bf16[2,192,256]{2,1,0:T(8,128)(2,1)S(1)}, u32[]{:S(2)}, u32[]{:S(2)}) %collective-permute-start) | collective-permute-done | bytes 196640 | tf_op jit(solution)/shard_map/while/body/eval_jaxpr/ppermute | solution.py:12
  151.8 8.4 %collective-permute-done = bf16[2,192,256]{2,1,0:T(8,128)(2,1)S(1)} collective-permute-done((bf16[2,192,256]{2,1,0:T(8,128)(2,1)S(1)}, bf16[2,192,256]{2,1,0:T(8,128)(2,1)S(1)}, u32[]{:S(2)}, u32[]{:S(2)}) %collective-permute-start) | collective-permute-done | bytes 196640 | tf_op jit(solution)/shard_map/while/body/eval_jaxpr/ppermute | solution.py:12
  160.3 3.1 copy.27
  163.3 3.9 %fusion.51 = (bf16[1,3072,256]{1,2,0:T(8,128)(2,1)}, bf16[1,3072,256]{1,2,0:T(8,128)(2,1)}) fusion(bf16[2,3072,256]{1,2,0:T(8,128)(2,1)} %copy.27), kind=kLoop, calls=%fused_computation.40 | loop fusion | bytes 6291456 | tf_op jit(solution)/shard_map/slice | solution.py:64
  168.6 143.1 %while.29 = (s32[]{:T(128)}, bf16[8,192,4,128]{3,1,2,0:T(8,128)(2,1)}, s32[8]{0:T(128)S(1)}, bf16[3072,2,128]{0,2,1:T(8,128)(2,1)}, bf16[3072,2,128]{0,2,1:T(8,1...) while((s32[]{:T(128)}, ...), condition=%wide.region_8.9_spmd.clone, body=%wide.region_5.8_spmd.clone.sunk | while | flops 1224084480 | bytes 13599102 | solution.py:73
  174.0 7.8 %fusion.62 = (f32[4,192]{1,0:T(4,128)S(1)}, bf16[4,192,3072]{2,1,0:T(8,128)(2,1)}) fusion(pred[192,3072]{1,0:T(8,128)(4,1)S(1)} %compare_and_fusion.2, bf16[3072,2,128]{0,2,1:T(8,128)(2,1)} %get-tuple-element.397, s32[]{:T(128)S(6)} %select_n.75, bf16[1,192,4,128]{3,2,0,1:T(4,128)(2,1)S(1)} %constant_dynamic-slice_fusion.2), kind=kOutput, calls=%fused_computation.39.clone.1 | convolution fusion | flops 618138624 | bytes 6884356 | tf_op jit(solution)/shard_map/while/body/eval_jaxpr/sub | solution.py:21
  181.8 4.6 %fusion.63 = bf16[8,192,4,128]{3,1,2,0:T(8,128)(2,1)} fusion(bf16[8,192,4,128]{3,1,2,0:T(8,128)(2,1)} %get-tuple-element.378, s32[]{:T(128)} %get-tuple-element.377, bf16[4,192,3072]{2,1,0:T(8,128)(2,1)} %get-tuple-element.335, bf16[3072,2,128]{0,2,1:T(8,128)(2,1)} %get-tuple-element.396, s32[]{:T(128)S(6)} %select_n.75, f32[192,4]{0,1:T(4,128)S(1)} %bitcast.94), kind=kOutput, calls=%fused_computation.17.clone.1 | convolution fusion | flops 604176384 | bytes 5705220 | tf_op jit(solution)/shard_map/while/body/eval_jaxpr/hqk,kd->qhd/dot_general | solution.py:24
  191.9 7.8 %fusion.62 = (f32[4,192]{1,0:T(4,128)S(1)}, bf16[4,192,3072]{2,1,0:T(8,128)(2,1)}) fusion(pred[192,3072]{1,0:T(8,128)(4,1)S(1)} %compare_and_fusion.2, bf16[3072,2,128]{0,2,1:T(8,128)(2,1)} %get-tuple-element.397, s32[]{:T(128)S(6)} %select_n.75, bf16[1,192,4,128]{3,2,0,1:T(4,128)(2,1)S(1)} %constant_dynamic-slice_fusion.2), kind=kOutput, calls=%fused_computation.39.clone.1 | convolution fusion | flops 618138624 | bytes 6884356 | tf_op jit(solution)/shard_map/while/body/eval_jaxpr/sub | solution.py:21
  199.7 4.6 %fusion.63 = bf16[8,192,4,128]{3,1,2,0:T(8,128)(2,1)} fusion(bf16[8,192,4,128]{3,1,2,0:T(8,128)(2,1)} %get-tuple-element.378, s32[]{:T(128)} %get-tuple-element.377, bf16[4,192,3072]{2,1,0:T(8,128)(2,1)} %get-tuple-element.335, bf16[3072,2,128]{0,2,1:T(8,128)(2,1)} %get-tuple-element.396, s32[]{:T(128)S(6)} %select_n.75, f32[192,4]{0,1:T(4,128)S(1)} %bitcast.94), kind=kOutput, calls=%fused_computation.17.clone.1 | convolution fusion | flops 604176384 | bytes 5705220 | tf_op jit(solution)/shard_map/while/body/eval_jaxpr/hqk,kd->qhd/dot_general | solution.py:24
  209.8 7.8 %fusion.62 = (f32[4,192]{1,0:T(4,128)S(1)}, bf16[4,192,3072]{2,1,0:T(8,128)(2,1)}) fusion(pred[192,3072]{1,0:T(8,128)(4,1)S(1)} %compare_and_fusion.2, bf16[3072,2,128]{0,2,1:T(8,128)(2,1)} %get-tuple-element.397, s32[]{:T(128)S(6)} %select_n.75, bf16[1,192,4,128]{3,2,0,1:T(4,128)(2,1)S(1)} %constant_dynamic-slice_fusion.2), kind=kOutput, calls=%fused_computation.39.clone.1 | convolution fusion | flops 618138624 | bytes 6884356 | tf_op jit(solution)/shard_map/while/body/eval_jaxpr/sub | solution.py:21
  217.6 4.6 %fusion.63 = bf16[8,192,4,128]{3,1,2,0:T(8,128)(2,1)} fusion(bf16[8,192,4,128]{3,1,2,0:T(8,128)(2,1)} %get-tuple-element.378, s32[]{:T(128)} %get-tuple-element.377, bf16[4,192,3072]{2,1,0:T(8,128)(2,1)} %get-tuple-element.335, bf16[3072,2,128]{0,2,1:T(8,128)(2,1)} %get-tuple-element.396, s32[]{:T(128)S(6)} %select_n.75, f32[192,4]{0,1:T(4,128)S(1)} %bitcast.94), kind=kOutput, calls=%fused_computation.17.clone.1 | convolution fusion | flops 604176384 | bytes 5705220 | tf_op jit(solution)/shard_map/while/body/eval_jaxpr/hqk,kd->qhd/dot_general | solution.py:24
  227.7 7.8 %fusion.62 = (f32[4,192]{1,0:T(4,128)S(1)}, bf16[4,192,3072]{2,1,0:T(8,128)(2,1)}) fusion(pred[192,3072]{1,0:T(8,128)(4,1)S(1)} %compare_and_fusion.2, bf16[3072,2,128]{0,2,1:T(8,128)(2,1)} %get-tuple-element.397, s32[]{:T(128)S(6)} %select_n.75, bf16[1,192,4,128]{3,2,0,1:T(4,128)(2,1)S(1)} %constant_dynamic-slice_fusion.2), kind=kOutput, calls=%fused_computation.39.clone.1 | convolution fusion | flops 618138624 | bytes 6884356 | tf_op jit(solution)/shard_map/while/body/eval_jaxpr/sub | solution.py:21
  235.5 4.6 %fusion.63 = bf16[8,192,4,128]{3,1,2,0:T(8,128)(2,1)} fusion(bf16[8,192,4,128]{3,1,2,0:T(8,128)(2,1)} %get-tuple-element.378, s32[]{:T(128)} %get-tuple-element.377, bf16[4,192,3072]{2,1,0:T(8,128)(2,1)} %get-tuple-element.335, bf16[3072,2,128]{0,2,1:T(8,128)(2,1)} %get-tuple-element.396, s32[]{:T(128)S(6)} %select_n.75, f32[192,4]{0,1:T(4,128)S(1)} %bitcast.94), kind=kOutput, calls=%fused_computation.17.clone.1 | convolution fusion | flops 604176384 | bytes 5705220 | tf_op jit(solution)/shard_map/while/body/eval_jaxpr/hqk,kd->qhd/dot_general | solution.py:24
  245.6 7.8 %fusion.62 = (f32[4,192]{1,0:T(4,128)S(1)}, bf16[4,192,3072]{2,1,0:T(8,128)(2,1)}) fusion(pred[192,3072]{1,0:T(8,128)(4,1)S(1)} %compare_and_fusion.2, bf16[3072,2,128]{0,2,1:T(8,128)(2,1)} %get-tuple-element.397, s32[]{:T(128)S(6)} %select_n.75, bf16[1,192,4,128]{3,2,0,1:T(4,128)(2,1)S(1)} %constant_dynamic-slice_fusion.2), kind=kOutput, calls=%fused_computation.39.clone.1 | convolution fusion | flops 618138624 | bytes 6884356 | tf_op jit(solution)/shard_map/while/body/eval_jaxpr/sub | solution.py:21
  253.4 4.6 %fusion.63 = bf16[8,192,4,128]{3,1,2,0:T(8,128)(2,1)} fusion(bf16[8,192,4,128]{3,1,2,0:T(8,128)(2,1)} %get-tuple-element.378, s32[]{:T(128)} %get-tuple-element.377, bf16[4,192,3072]{2,1,0:T(8,128)(2,1)} %get-tuple-element.335, bf16[3072,2,128]{0,2,1:T(8,128)(2,1)} %get-tuple-element.396, s32[]{:T(128)S(6)} %select_n.75, f32[192,4]{0,1:T(4,128)S(1)} %bitcast.94), kind=kOutput, calls=%fused_computation.17.clone.1 | convolution fusion | flops 604176384 | bytes 5705220 | tf_op jit(solution)/shard_map/while/body/eval_jaxpr/hqk,kd->qhd/dot_general | solution.py:24
  263.5 7.8 %fusion.62 = (f32[4,192]{1,0:T(4,128)S(1)}, bf16[4,192,3072]{2,1,0:T(8,128)(2,1)}) fusion(pred[192,3072]{1,0:T(8,128)(4,1)S(1)} %compare_and_fusion.2, bf16[3072,2,128]{0,2,1:T(8,128)(2,1)} %get-tuple-element.397, s32[]{:T(128)S(6)} %select_n.75, bf16[1,192,4,128]{3,2,0,1:T(4,128)(2,1)S(1)} %constant_dynamic-slice_fusion.2), kind=kOutput, calls=%fused_computation.39.clone.1 | convolution fusion | flops 618138624 | bytes 6884356 | tf_op jit(solution)/shard_map/while/body/eval_jaxpr/sub | solution.py:21
  271.3 4.6 %fusion.63 = bf16[8,192,4,128]{3,1,2,0:T(8,128)(2,1)} fusion(bf16[8,192,4,128]{3,1,2,0:T(8,128)(2,1)} %get-tuple-element.378, s32[]{:T(128)} %get-tuple-element.377, bf16[4,192,3072]{2,1,0:T(8,128)(2,1)} %get-tuple-element.335, bf16[3072,2,128]{0,2,1:T(8,128)(2,1)} %get-tuple-element.396, s32[]{:T(128)S(6)} %select_n.75, f32[192,4]{0,1:T(4,128)S(1)} %bitcast.94), kind=kOutput, calls=%fused_computation.17.clone.1 | convolution fusion | flops 604176384 | bytes 5705220 | tf_op jit(solution)/shard_map/while/body/eval_jaxpr/hqk,kd->qhd/dot_general | solution.py:24
  281.3 7.8 %fusion.62 = (f32[4,192]{1,0:T(4,128)S(1)}, bf16[4,192,3072]{2,1,0:T(8,128)(2,1)}) fusion(pred[192,3072]{1,0:T(8,128)(4,1)S(1)} %compare_and_fusion.2, bf16[3072,2,128]{0,2,1:T(8,128)(2,1)} %get-tuple-element.397, s32[]{:T(128)S(6)} %select_n.75, bf16[1,192,4,128]{3,2,0,1:T(4,128)(2,1)S(1)} %constant_dynamic-slice_fusion.2), kind=kOutput, calls=%fused_computation.39.clone.1 | convolution fusion | flops 618138624 | bytes 6884356 | tf_op jit(solution)/shard_map/while/body/eval_jaxpr/sub | solution.py:21
  289.1 4.6 %fusion.63 = bf16[8,192,4,128]{3,1,2,0:T(8,128)(2,1)} fusion(bf16[8,192,4,128]{3,1,2,0:T(8,128)(2,1)} %get-tuple-element.378, s32[]{:T(128)} %get-tuple-element.377, bf16[4,192,3072]{2,1,0:T(8,128)(2,1)} %get-tuple-element.335, bf16[3072,2,128]{0,2,1:T(8,128)(2,1)} %get-tuple-element.396, s32[]{:T(128)S(6)} %select_n.75, f32[192,4]{0,1:T(4,128)S(1)} %bitcast.94), kind=kOutput, calls=%fused_computation.17.clone.1 | convolution fusion | flops 604176384 | bytes 5705220 | tf_op jit(solution)/shard_map/while/body/eval_jaxpr/hqk,kd->qhd/dot_general | solution.py:24
  299.2 7.8 %fusion.62 = (f32[4,192]{1,0:T(4,128)S(1)}, bf16[4,192,3072]{2,1,0:T(8,128)(2,1)}) fusion(pred[192,3072]{1,0:T(8,128)(4,1)S(1)} %compare_and_fusion.2, bf16[3072,2,128]{0,2,1:T(8,128)(2,1)} %get-tuple-element.397, s32[]{:T(128)S(6)} %select_n.75, bf16[1,192,4,128]{3,2,0,1:T(4,128)(2,1)S(1)} %constant_dynamic-slice_fusion.2), kind=kOutput, calls=%fused_computation.39.clone.1 | convolution fusion | flops 618138624 | bytes 6884356 | tf_op jit(solution)/shard_map/while/body/eval_jaxpr/sub | solution.py:21
  307.0 4.6 %fusion.63 = bf16[8,192,4,128]{3,1,2,0:T(8,128)(2,1)} fusion(bf16[8,192,4,128]{3,1,2,0:T(8,128)(2,1)} %get-tuple-element.378, s32[]{:T(128)} %get-tuple-element.377, bf16[4,192,3072]{2,1,0:T(8,128)(2,1)} %get-tuple-element.335, bf16[3072,2,128]{0,2,1:T(8,128)(2,1)} %get-tuple-element.396, s32[]{:T(128)S(6)} %select_n.75, f32[192,4]{0,1:T(4,128)S(1)} %bitcast.94), kind=kOutput, calls=%fused_computation.17.clone.1 | convolution fusion | flops 604176384 | bytes 5705220 | tf_op jit(solution)/shard_map/while/body/eval_jaxpr/hqk,kd->qhd/dot_general | solution.py:24
  315.2 18.2 %all_to_all.5 = bf16[4,48,4096]{2,1,0:T(8,128)(2,1)S(1)} all-to-all(bf16[4,48,4096]{2,1,0:T(8,128)(2,1)S(1)} %pad_maximum_fusion), channel_id=1, replica_groups=mesh['ctx'=64,'head'=4] {'head'}, dimensions={0} | all-to-all | bytes 3145728 | tf_op jit(solution)/shard_map/all_to_all | solution.py:78
  (85 shorter events, 27.1 us)
Async XLA Ops:
  4.7 10.3 %collective-permute-start = (bf16[2,192,256]{2,1,0:T(8,128)(2,1)S(1)}, bf16[2,192,256]{2,1,0:T(8,128)(2,1)S(1)}, u32[]{:S(2)}, u32[]{:S(2)}) collective-permute-start(bf16[2,192,256]{2,1,0:T(8,128)(2,1)S(1)} %get-tuple-element.347), channel_id=1, source_target_pairs={{0,4},{4,8},{8,12},{12,16},{16,20},{20,24},{24,28},{28,32},{32,36}... | collective-permute-start | bytes 589832 | tf_op jit(solution)/shard_map/while/body/eval_jaxpr/ppermute | solution.py:12
  15.1 10.3 %collective-permute-start = (bf16[2,192,256]{2,1,0:T(8,128)(2,1)S(1)}, bf16[2,192,256]{2,1,0:T(8,128)(2,1)S(1)}, u32[]{:S(2)}, u32[]{:S(2)}) collective-permute-start(bf16[2,192,256]{2,1,0:T(8,128)(2,1)S(1)} %get-tuple-element.347), channel_id=1, source_target_pairs={{0,4},{4,8},{8,12},{12,16},{16,20},{20,24},{24,28},{28,32},{32,36}... | collective-permute-start | bytes 589832 | tf_op jit(solution)/shard_map/while/body/eval_jaxpr/ppermute | solution.py:12
  25.5 10.3 %collective-permute-start = (bf16[2,192,256]{2,1,0:T(8,128)(2,1)S(1)}, bf16[2,192,256]{2,1,0:T(8,128)(2,1)S(1)}, u32[]{:S(2)}, u32[]{:S(2)}) collective-permute-start(bf16[2,192,256]{2,1,0:T(8,128)(2,1)S(1)} %get-tuple-element.347), channel_id=1, source_target_pairs={{0,4},{4,8},{8,12},{12,16},{16,20},{20,24},{24,28},{28,32},{32,36}... | collective-permute-start | bytes 589832 | tf_op jit(solution)/shard_map/while/body/eval_jaxpr/ppermute | solution.py:12
  35.8 10.3 %collective-permute-start = (bf16[2,192,256]{2,1,0:T(8,128)(2,1)S(1)}, bf16[2,192,256]{2,1,0:T(8,128)(2,1)S(1)}, u32[]{:S(2)}, u32[]{:S(2)}) collective-permute-start(bf16[2,192,256]{2,1,0:T(8,128)(2,1)S(1)} %get-tuple-element.347), channel_id=1, source_target_pairs={{0,4},{4,8},{8,12},{12,16},{16,20},{20,24},{24,28},{28,32},{32,36}... | collective-permute-start | bytes 589832 | tf_op jit(solution)/shard_map/while/body/eval_jaxpr/ppermute | solution.py:12
  46.2 10.3 %collective-permute-start = (bf16[2,192,256]{2,1,0:T(8,128)(2,1)S(1)}, bf16[2,192,256]{2,1,0:T(8,128)(2,1)S(1)}, u32[]{:S(2)}, u32[]{:S(2)}) collective-permute-start(bf16[2,192,256]{2,1,0:T(8,128)(2,1)S(1)} %get-tuple-element.347), channel_id=1, source_target_pairs={{0,4},{4,8},{8,12},{12,16},{16,20},{20,24},{24,28},{28,32},{32,36}... | collective-permute-start | bytes 589832 | tf_op jit(solution)/shard_map/while/body/eval_jaxpr/ppermute | solution.py:12
  56.6 10.3 %collective-permute-start = (bf16[2,192,256]{2,1,0:T(8,128)(2,1)S(1)}, bf16[2,192,256]{2,1,0:T(8,128)(2,1)S(1)}, u32[]{:S(2)}, u32[]{:S(2)}) collective-permute-start(bf16[2,192,256]{2,1,0:T(8,128)(2,1)S(1)} %get-tuple-element.347), channel_id=1, source_target_pairs={{0,4},{4,8},{8,12},{12,16},{16,20},{20,24},{24,28},{28,32},{32,36}... | collective-permute-start | bytes 589832 | tf_op jit(solution)/shard_map/while/body/eval_jaxpr/ppermute | solution.py:12
  66.9 10.3 %collective-permute-start = (bf16[2,192,256]{2,1,0:T(8,128)(2,1)S(1)}, bf16[2,192,256]{2,1,0:T(8,128)(2,1)S(1)}, u32[]{:S(2)}, u32[]{:S(2)}) collective-permute-start(bf16[2,192,256]{2,1,0:T(8,128)(2,1)S(1)} %get-tuple-element.347), channel_id=1, source_target_pairs={{0,4},{4,8},{8,12},{12,16},{16,20},{20,24},{24,28},{28,32},{32,36}... | collective-permute-start | bytes 589832 | tf_op jit(solution)/shard_map/while/body/eval_jaxpr/ppermute | solution.py:12
  77.3 10.3 %collective-permute-start = (bf16[2,192,256]{2,1,0:T(8,128)(2,1)S(1)}, bf16[2,192,256]{2,1,0:T(8,128)(2,1)S(1)}, u32[]{:S(2)}, u32[]{:S(2)}) collective-permute-start(bf16[2,192,256]{2,1,0:T(8,128)(2,1)S(1)} %get-tuple-element.347), channel_id=1, source_target_pairs={{0,4},{4,8},{8,12},{12,16},{16,20},{20,24},{24,28},{28,32},{32,36}... | collective-permute-start | bytes 589832 | tf_op jit(solution)/shard_map/while/body/eval_jaxpr/ppermute | solution.py:12
  87.7 10.3 %collective-permute-start = (bf16[2,192,256]{2,1,0:T(8,128)(2,1)S(1)}, bf16[2,192,256]{2,1,0:T(8,128)(2,1)S(1)}, u32[]{:S(2)}, u32[]{:S(2)}) collective-permute-start(bf16[2,192,256]{2,1,0:T(8,128)(2,1)S(1)} %get-tuple-element.347), channel_id=1, source_target_pairs={{0,4},{4,8},{8,12},{12,16},{16,20},{20,24},{24,28},{28,32},{32,36}... | collective-permute-start | bytes 589832 | tf_op jit(solution)/shard_map/while/body/eval_jaxpr/ppermute | solution.py:12
  98.0 10.3 %collective-permute-start = (bf16[2,192,256]{2,1,0:T(8,128)(2,1)S(1)}, bf16[2,192,256]{2,1,0:T(8,128)(2,1)S(1)}, u32[]{:S(2)}, u32[]{:S(2)}) collective-permute-start(bf16[2,192,256]{2,1,0:T(8,128)(2,1)S(1)} %get-tuple-element.347), channel_id=1, source_target_pairs={{0,4},{4,8},{8,12},{12,16},{16,20},{20,24},{24,28},{28,32},{32,36}... | collective-permute-start | bytes 589832 | tf_op jit(solution)/shard_map/while/body/eval_jaxpr/ppermute | solution.py:12
  108.4 10.3 %collective-permute-start = (bf16[2,192,256]{2,1,0:T(8,128)(2,1)S(1)}, bf16[2,192,256]{2,1,0:T(8,128)(2,1)S(1)}, u32[]{:S(2)}, u32[]{:S(2)}) collective-permute-start(bf16[2,192,256]{2,1,0:T(8,128)(2,1)S(1)} %get-tuple-element.347), channel_id=1, source_target_pairs={{0,4},{4,8},{8,12},{12,16},{16,20},{20,24},{24,28},{28,32},{32,36}... | collective-permute-start | bytes 589832 | tf_op jit(solution)/shard_map/while/body/eval_jaxpr/ppermute | solution.py:12
  118.8 10.3 %collective-permute-start = (bf16[2,192,256]{2,1,0:T(8,128)(2,1)S(1)}, bf16[2,192,256]{2,1,0:T(8,128)(2,1)S(1)}, u32[]{:S(2)}, u32[]{:S(2)}) collective-permute-start(bf16[2,192,256]{2,1,0:T(8,128)(2,1)S(1)} %get-tuple-element.347), channel_id=1, source_target_pairs={{0,4},{4,8},{8,12},{12,16},{16,20},{20,24},{24,28},{28,32},{32,36}... | collective-permute-start | bytes 589832 | tf_op jit(solution)/shard_map/while/body/eval_jaxpr/ppermute | solution.py:12
  129.2 10.3 %collective-permute-start = (bf16[2,192,256]{2,1,0:T(8,128)(2,1)S(1)}, bf16[2,192,256]{2,1,0:T(8,128)(2,1)S(1)}, u32[]{:S(2)}, u32[]{:S(2)}) collective-permute-start(bf16[2,192,256]{2,1,0:T(8,128)(2,1)S(1)} %get-tuple-element.347), channel_id=1, source_target_pairs={{0,4},{4,8},{8,12},{12,16},{16,20},{20,24},{24,28},{28,32},{32,36}... | collective-permute-start | bytes 589832 | tf_op jit(solution)/shard_map/while/body/eval_jaxpr/ppermute | solution.py:12
  139.5 10.3 %collective-permute-start = (bf16[2,192,256]{2,1,0:T(8,128)(2,1)S(1)}, bf16[2,192,256]{2,1,0:T(8,128)(2,1)S(1)}, u32[]{:S(2)}, u32[]{:S(2)}) collective-permute-start(bf16[2,192,256]{2,1,0:T(8,128)(2,1)S(1)} %get-tuple-element.347), channel_id=1, source_target_pairs={{0,4},{4,8},{8,12},{12,16},{16,20},{20,24},{24,28},{28,32},{32,36}... | collective-permute-start | bytes 589832 | tf_op jit(solution)/shard_map/while/body/eval_jaxpr/ppermute | solution.py:12
  149.9 10.3 %collective-permute-start = (bf16[2,192,256]{2,1,0:T(8,128)(2,1)S(1)}, bf16[2,192,256]{2,1,0:T(8,128)(2,1)S(1)}, u32[]{:S(2)}, u32[]{:S(2)}) collective-permute-start(bf16[2,192,256]{2,1,0:T(8,128)(2,1)S(1)} %get-tuple-element.347), channel_id=1, source_target_pairs={{0,4},{4,8},{8,12},{12,16},{16,20},{20,24},{24,28},{28,32},{32,36}... | collective-permute-start | bytes 589832 | tf_op jit(solution)/shard_map/while/body/eval_jaxpr/ppermute | solution.py:12
  163.3 4.1 %copy-start = (bf16[192,4096]{1,0:T(8,128)(2,1)S(1)}, bf16[192,4096]{1,0:T(8,128)(2,1)}, u32[]{:S(2)}) copy-start(bf16[192,4096]{1,0:T(8,128)(2,1)} %param.8) | copy-start | bytes 4718596
  167.4 1.2 copy-start.1
